TPU v7x, 32 devices: a whole 2x2x4 slice. The times are simulated.
32 devices in a mesh: blk: 16 (over z, x, core), partner: 2 (over y).
Axes of the slice: x: 2, y: 2, z: 4, core: 2. Of those that a mesh axis runs over, the one named last changes fastest.
Arguments:
- a_blocks: bfloat16 [16384, 3072], P(('blk', 'partner')), may hold values from -0.75 to 0.75
- p_blocks: bfloat16 [256, 4096], P(('blk', 'partner')), may hold values from -0.75 to 0.75
- agg_ids: int32 [256], P(('blk', 'partner')), may hold values from 0 to 3
- cols: int32 [256, 48], P(('blk', 'partner')), may hold values from 0 to 7
- counts: int32 [256, 8], P(('blk', 'partner')), may hold values from 0 to 6, as said below
Outputs:
- coarse: float32 [64, 64, 2048], P('blk', 'partner')
Inputs may be any that keep to these rules, and one draw needn't show every extreme that they name: `cols`: a slot's row index within the device that owns its block column. `agg_ids`: an aggregate within the row's sector. The live blocks of a row for one sector offset are its first counts slots of that offset; some rows use all 6 of them.
All inputs are finite; a program needn't handle non-finite values.
Results may differ from a plain program's by a relative error of at most 0.0029.
Values may be sent and summed in bfloat16 or wider, within the bound.
A program may use at most 64 MiB of HBM per device.

v0:
```python
import functools

import jax
import jax.numpy as jnp
from jax import lax
from jax.experimental import pallas as pl
from jax.experimental.pallas import tpu as pltpu
from jax.sharding import PartitionSpec as P

BLOCK = 64
AGG = 4
MESH = pl.DeviceIdType.MESH
WIDE = AGG * BLOCK


def offset_of(step):
    return (1 - 2 * (step % 2)) * ((step + 1) // 2)


def kernel(n_blk, n_partner, rows, window, pairs,
           a_ref, p_ref, code_ref, out_ref,
           panels, own_t, spread, pd, parts, sent, got,
           panel_send, panel_recv, part_send, part_recv):
    me = lax.axis_index("blk")
    mine = lax.axis_index("partner")
    height = BLOCK // n_partner
    columns = rows // 2

    barrier = pltpu.get_barrier_semaphore()
    for step in range(1, window):
        source = lax.rem(me + offset_of(step) + n_blk, n_blk)
        pl.semaphore_signal(barrier, inc=1, device_id=(source, mine), device_id_type=MESH)
    for d in range(1, n_partner):
        pl.semaphore_signal(barrier, inc=1, device_id=(me, lax.rem(mine + d, n_partner)), device_id_type=MESH)
    pl.semaphore_wait(barrier, window - 1 + n_partner - 1)

    def panel_copy(step):
        return pltpu.make_async_remote_copy(
            src_ref=p_ref,
            dst_ref=panels.at[step],
            send_sem=panel_send.at[step],
            recv_sem=panel_recv.at[step],
            device_id=(lax.rem(me - offset_of(step) + n_blk, n_blk), mine),
            device_id_type=MESH,
        )

    def part_copy(step, d):
        to = lax.rem(mine + d, n_partner)
        return pltpu.make_async_remote_copy(
            src_ref=sent.at[step, to],
            dst_ref=got.at[step, d - 1],
            send_sem=part_send.at[step, d - 1],
            recv_sem=part_recv.at[step, d - 1],
            device_id=(me, to),
            device_id_type=MESH,
        )

    for step in range(1, window):
        panel_copy(step).start()

    upper = (lax.broadcasted_iota(jnp.int32, (8, 2 * BLOCK), 1) >= BLOCK).astype(jnp.float32)
    upper_row = upper[0:1]

    def place(panel):
        packed = panel[: columns * BLOCK].astype(jnp.float32)
        masks = panel[columns * BLOCK :].astype(jnp.float32)
        turned = pltpu.roll(packed, BLOCK, 1)
        for half, both in enumerate((packed * (1 - upper_row) + turned * upper_row,
                                     turned * (1 - upper_row) + packed * upper_row)):
            for column in range(columns):
                block = both[column * BLOCK : (column + 1) * BLOCK]
                row = column + half * columns
                for tile in range(2):
                    mask = masks[tile * rows + row : tile * rows + row + 1]
                    pd[row * BLOCK : (row + 1) * BLOCK, tile * 2 * BLOCK : (tile + 1) * 2 * BLOCK] = (
                        block * mask
                    ).astype(jnp.bfloat16)

    place(p_ref[...])
    own_t[...] = pd[...].astype(jnp.float32).T.astype(jnp.bfloat16)

    def one_step(step, carry):
        index = offset_of(step) + window // 2

        def one_row(g, inner):
            code = code_ref[index * rows + g]
            first = pl.multiple_of(g * BLOCK, BLOCK)
            straight = []
            for k in range(pairs):
                start = pl.multiple_of((index * pairs + k) * 2 * BLOCK, 2 * BLOCK)
                tile = a_ref[pl.ds(first, BLOCK), pl.ds(start, 2 * BLOCK)].astype(jnp.float32)
                straight.append(tile)
            tiles = straight + [pltpu.roll(tile, BLOCK, 1) for tile in straight]
            for m in range(columns):
                weight = jnp.where(code == upper + 2.0 * m, 1.0, 0.0)
                total = tiles[0] * weight[0:1]
                for r in range(1, 2 * pairs):
                    total = total + tiles[r] * weight[r : r + 1]
                spread[pl.ds(first, BLOCK), m * 2 * BLOCK : (m + 1) * 2 * BLOCK] = total.astype(jnp.bfloat16)
            return inner

        lax.fori_loop(0, rows, one_row, 0)

        @pl.when(step > 0)
        def _():
            panel_copy(step).wait_recv()
            place(panels[step])

        product = jnp.dot(spread[...], pd[...], preferred_element_type=jnp.float32)
        top = product.astype(jnp.bfloat16)
        rest = (product - top.astype(jnp.float32)).astype(jnp.bfloat16)
        coarse = jnp.dot(own_t[...], top, preferred_element_type=jnp.float32)
        coarse = coarse + jnp.dot(own_t[...], rest, preferred_element_type=jnp.float32)
        for q in range(n_partner):
            part = jnp.concatenate(
                [coarse[i * BLOCK + q * height : i * BLOCK + (q + 1) * height] for i in range(AGG)], axis=0
            )
            parts[step, q] = part
            sent[step, q] = part.astype(jnp.bfloat16)
        for d in range(1, n_partner):
            part_copy(step, d).start()
        return carry

    lax.fori_loop(0, window, one_step, 0)

    def finish(step, carry):
        index = offset_of(step) + window // 2
        total = parts[step, mine]
        for d in range(1, n_partner):
            part_copy(step, d).wait_recv()
            total = total + got[step, d - 1].astype(jnp.float32)
        start = pl.multiple_of(index * WIDE, WIDE)
        for i in range(AGG):
            out_ref[i, :, pl.ds(start, WIDE)] = total[i * height : (i + 1) * height]
        return carry

    lax.fori_loop(0, window, finish, 0)
    for step in range(1, window):
        panel_copy(step).wait_send()
    for step in range(window):
        for d in range(1, n_partner):
            part_copy(step, d).wait_send()


def on_device(n_blk, n_partner, a_blocks, p_blocks, agg_ids, cols, counts):
    rows = p_blocks.shape[0]
    window = counts.shape[1]
    kper = cols.shape[1] // window
    pairs = kper // 2
    columns = rows // 2
    height = BLOCK // n_partner
    packed = p_blocks.reshape(2, columns, BLOCK, BLOCK).transpose(1, 2, 0, 3).reshape(columns * BLOCK, 2 * BLOCK)
    lane = jnp.arange(WIDE, dtype=jnp.int32) // BLOCK
    masks = (agg_ids[None, :, None] == lane.reshape(2, 1, 2 * BLOCK)).reshape(2 * rows, 2 * BLOCK)
    panel = jnp.concatenate([packed, masks.astype(jnp.bfloat16)], axis=0)

    live = jnp.arange(kper, dtype=jnp.int32) < counts[:, :, None]
    code = jnp.where(live, cols.reshape(rows, window, kper), -4).astype(jnp.float32)
    code = code.transpose(1, 0, 2).reshape(window * rows, pairs, 2)
    code = jnp.concatenate([code, code[:, :, ::-1]], axis=1)
    code = jnp.pad(code, ((0, 0), (0, 8 - 2 * pairs), (0, 0)), constant_values=-4.0)
    code = jnp.repeat(code, BLOCK, axis=2)

    vmem = pl.BlockSpec(memory_space=pltpu.VMEM)
    size = rows * BLOCK
    return pl.pallas_call(
        functools.partial(kernel, n_blk, n_partner, rows, window, pairs),
        out_shape=jax.ShapeDtypeStruct((AGG, height, window * WIDE), jnp.float32),
        in_specs=[vmem] * 3,
        out_specs=vmem,
        scratch_shapes=[
            pltpu.VMEM((window,) + panel.shape, jnp.bfloat16),
            pltpu.VMEM((WIDE, size), jnp.bfloat16),
            pltpu.VMEM((size, size), jnp.bfloat16),
            pltpu.VMEM((size, WIDE), jnp.bfloat16),
            pltpu.VMEM((window, n_partner, AGG * height, WIDE), jnp.float32),
            pltpu.VMEM((window, n_partner, AGG * height, WIDE), jnp.bfloat16),
            pltpu.VMEM((window, max(n_partner - 1, 1), AGG * height, WIDE), jnp.bfloat16),
            pltpu.SemaphoreType.DMA((window,)),
            pltpu.SemaphoreType.DMA((window,)),
            pltpu.SemaphoreType.DMA((window, max(n_partner - 1, 1))),
            pltpu.SemaphoreType.DMA((window, max(n_partner - 1, 1))),
        ],
        compiler_params=pltpu.CompilerParams(
            collective_id=0, has_side_effects=True, vmem_limit_bytes=40 * 1024 * 1024
        ),
        cost_estimate=pl.CostEstimate(flops=3 * 10**9, bytes_accessed=5 * 10**6, transcendentals=0),
    )(a_blocks, panel, code)


def solution(mesh):
    placed = (
        P(("blk", "partner"), None),
        P(("blk", "partner"), None),
        P(("blk", "partner")),
        P(("blk", "partner"), None),
        P(("blk", "partner"), None),
    )
    return jax.shard_map(
        functools.partial(on_device, mesh.shape["blk"], mesh.shape["partner"]),
        mesh=mesh, in_specs=placed, out_specs=P("blk", "partner", None), check_vma=False,
    )
```

profile of v0, /device:TPU:0, one launch (start us, length us, event | category | flops | bytes accessed | tf_op | source)
XLA Modules:
  0.0 32.9 jit_solution(12641677840011495476)
XLA Ops:
  0.0 0.0 copy-start
  0.0 0.8 %eq.20 = s32[2,8]{1,0:T(2,128)S(1)} broadcast(s32[8]{0:T(128)} %param.7), dimensions={1} | broadcast | bytes 96 | tf_op jit(solution)/shard_map/eq | solution.py:154
  0.8 0.1 eq.21
  0.9 0.1 fusion
  1.0 0.8 %reshape.51 = s32[8,8,6]{2,1,0:T(8,128)S(1)} reshape(s32[8,48]{1,0:T(8,128)} %param.8) | data formatting | bytes 3072 | tf_op jit(solution)/shard_map/reshape | solution.py:158
  1.7 0.8 %convert_bitcast_fusion = f32[8,8,6]{2,0,1:T(8,128)S(1)} fusion(s32[8,8,6]{2,1,0:T(8,128)S(1)} %reshape.51, s32[8,8]{1,0:T(8,128)} %param.9), kind=kLoop, calls=%fused_computation.2 | loop fusion | flops 1152 | bytes 3328 | tf_op jit(solution)/shard_map/transpose | solution.py:159
  2.5 0.1 copy.8
  2.6 0.1 reshape.52
  2.8 1.0 %reshape.49 = bf16[2,4,64,64]{3,2,1,0:T(8,128)(2,1)S(1)} reshape(bf16[8,4096]{1,0:T(8,128)(2,1)} %param.6) | data formatting | bytes 131072 | tf_op jit(solution)/shard_map/reshape | solution.py:152
  3.8 0.1 copy.12
  4.0 0.1 reshape.50
  4.1 0.2 copy.10
  4.3 1.4 %broadcast_in_dim.11 = f32[64,8,2,64]{3,2,1,0:T(2,128)} broadcast(f32[64,8,2]{2,1,0:T(8,128)S(1)} %pad.4.clone), dimensions={0,1,2} | broadcast | bytes 266240 | tf_op jit(solution)/shard_map/broadcast_in_dim | solution.py:162
  5.7 1.3 %reshape.53.code_ref = f32[64,8,128]{2,1,0:T(8,128)S(1)} reshape(f32[64,8,2,64]{3,2,1,0:T(2,128)} %broadcast_in_dim.11) | data formatting | bytes 524288 | tf_op jit(solution)/shard_map/reshape | solution.py:162
  7.0 0.0 copy-done
  7.0 24.9 %shard_map.55 = f32[4,32,2048]{2,1,0:T(8,128)S(1)} custom-call(bf16[512,3072]{1,0:T(8,128)(2,1)S(1)} %copy-done, bf16[272,128]{1,0:T(8,128)(2,1)S(1)} %pad_maximum_fusion.p_ref, f32[64,8,128]{2,1,0:T(8,128)S(1)} %reshape.53.code_ref), custom_call_target="tpu_custom_call" | custom-call | flops 3000000000 | bytes 5000000 | tf_op jit(solution)/shard_map/pallas_call | solution.py:166
  32.0 1.0 %copy.14 = f32[4,32,2048]{2,1,0:T(8,128)} copy(f32[4,32,2048]{2,1,0:T(8,128)S(1)} %shard_map.55) | data formatting | bytes 2097152
  (5 shorter events, 0.1 us)
Async XLA Ops:
  0.0 7.0 %copy-start = (bf16[512,3072]{1,0:T(8,128)(2,1)S(1)}, bf16[512,3072]{1,0:T(8,128)(2,1)}, u32[]{:S(2)}) copy-start(bf16[512,3072]{1,0:T(8,128)(2,1)} %a_ref.1) | copy-start | bytes 9437188
where the time goes:
time: 33.2 us; the launch traced here: 32.9 us
  Pallas kernels  24.9 us (75%)
  local copies, waits for them, and re-layouts  7.08 us (21%)
  other arithmetic  0.87 us (3%)
    pallas_call x1, Pallas kernels, on_device(): pl.pallas_call(functools.partial(kernel, n_blk, n_partner, rows, window,...  24.9 us
    broadcast_in_dim x1, local copies, waits for them, and re-layouts, on_device(): code = jnp.repeat(code, BLOCK, axis=2)  1.4 us
    reshape x1, local copies, waits for them, and re-layouts, on_device(): code = jnp.repeat(code, BLOCK, axis=2)  1.34 us
    reshape x3, local copies, waits for them, and re-layouts, on_device(): p_blocks.reshape(2, columns, BLOCK, BLOCK).transpose(1, 2, 0, 3)  1.28 us
    unnamed x4, local copies, waits for them, and re-layouts  1.15 us
    eq x2, local copies, waits for them, and re-layouts, on_device(): agg_ids[None, :, None] == lane.reshape(2, 1, 2 * BLOCK)  0.89 us
    transpose x1, other arithmetic, on_device(): code = code.transpose(1, 0, 2).reshape(window * rows, pairs, 2)  0.76 us
    reshape x1, local copies, waits for them, and re-layouts, on_device(): cols.reshape(rows, window, kper)  0.76 us

commit v1 on v0

v1 whole, which is shorter than its diff:
```python
import functools

import jax
import jax.numpy as jnp
from jax import lax
from jax.experimental import pallas as pl
from jax.experimental.pallas import tpu as pltpu
from jax.sharding import PartitionSpec as P

BLOCK = 64
AGG = 4
MESH = pl.DeviceIdType.MESH
WIDE = AGG * BLOCK


def offset_of(step):
    return (1 - 2 * (step % 2)) * ((step + 1) // 2)


def kernel(n_blk, n_partner, rows, window, kper,
           a_ref, p_ref, agg_ref, cols_ref, counts_ref, out_ref,
           a_slabs, panels, codes, raw, own_t, spread, placed, pd, parts, sent, got,
           slab_sem, panel_send, panel_recv, part_send, part_recv):
    me = lax.axis_index("blk")
    mine = lax.axis_index("partner")
    height = BLOCK // n_partner
    columns = rows // 2
    pairs = kper // 2
    wide = 2 * BLOCK
    packs = BLOCK // 2

    barrier = pltpu.get_barrier_semaphore()
    for step in range(1, window):
        source = lax.rem(me + offset_of(step) + n_blk, n_blk)
        pl.semaphore_signal(barrier, inc=1, device_id=(source, mine), device_id_type=MESH)
    for d in range(1, n_partner):
        pl.semaphore_signal(barrier, inc=1, device_id=(me, lax.rem(mine + d, n_partner)), device_id_type=MESH)

    def slab_copy(step):
        index = offset_of(step) + window // 2
        start = pl.multiple_of(index * (kper * BLOCK), wide)
        return pltpu.make_async_copy(
            a_ref.at[:, pl.ds(start, kper * BLOCK)], a_slabs.at[step], slab_sem.at[step]
        )

    for step in range(window):
        slab_copy(step).start()

    own = p_ref[...].astype(jnp.float32)
    for t in range(packs):
        raw[:, t, :] = own[:, t * wide : (t + 1) * wide]
    panels[0, : rows * packs, :] = raw[...].reshape(rows * packs, wide).astype(jnp.bfloat16)
    which = lax.broadcasted_iota(jnp.int32, (2 * rows, wide), 0)
    block_of = lax.broadcasted_iota(jnp.int32, (2 * rows, wide), 1) // BLOCK + 2 * (which // rows)
    aggregate = jnp.zeros((2 * rows, wide), jnp.int32)
    for g in range(rows):
        aggregate = jnp.where(which % rows == g, agg_ref[g], aggregate)
    panels[0, rows * packs :, :] = jnp.where(block_of == aggregate, 1.0, 0.0).astype(jnp.bfloat16)

    slots = window * kper
    for step in range(window):
        first = step * kper
        lane_slot = lax.broadcasted_iota(jnp.int32, (slots, kper * BLOCK), 1) // BLOCK
        chosen = lax.broadcasted_iota(jnp.int32, (slots, kper * BLOCK), 0) == lane_slot + first
        code = jnp.dot(cols_ref[...].astype(jnp.bfloat16), jnp.where(chosen, 1.0, 0.0).astype(jnp.bfloat16),
                       preferred_element_type=jnp.float32)
        order = lax.broadcasted_iota(jnp.int32, (rows, kper * BLOCK), 1) // BLOCK
        code = jnp.where(order < counts_ref[:, step : step + 1], code, -4.0)
        for k in range(pairs):
            straight = code[:, k * wide : (k + 1) * wide]
            for side, values in enumerate((straight, pltpu.roll(straight, BLOCK, 1))):
                for g in range(rows):
                    codes[step, g, 2 * k + side] = jnp.broadcast_to(values[g : g + 1], (8, wide))

    pl.semaphore_wait(barrier, window - 1 + n_partner - 1)

    def panel_copy(step):
        return pltpu.make_async_remote_copy(
            src_ref=panels.at[0],
            dst_ref=panels.at[step],
            send_sem=panel_send.at[step],
            recv_sem=panel_recv.at[step],
            device_id=(lax.rem(me - offset_of(step) + n_blk, n_blk), mine),
            device_id_type=MESH,
        )

    def part_copy(step, d):
        to = lax.rem(mine + d, n_partner)
        return pltpu.make_async_remote_copy(
            src_ref=sent.at[step, to],
            dst_ref=got.at[step, d - 1],
            send_sem=part_send.at[step, d - 1],
            recv_sem=part_recv.at[step, d - 1],
            device_id=(me, to),
            device_id_type=MESH,
        )

    for step in range(1, window):
        panel_copy(step).start()

    upper = (lax.broadcasted_iota(jnp.int32, (8, wide), 1) >= BLOCK).astype(jnp.float32)
    upper_row = upper[0:1]
    lower_row = 1 - upper_row

    def place(panel):
        packed = panel[: rows * packs].astype(jnp.float32)
        masks = panel[rows * packs :].astype(jnp.float32)
        turned = pltpu.roll(packed, BLOCK, 1)
        for half, both in enumerate((packed * lower_row + turned * upper_row, turned * lower_row + packed * upper_row)):
            for row in range(rows):
                block = both[row * packs : (row + 1) * packs]
                for tile in range(2):
                    mask = masks[tile * rows + row : tile * rows + row + 1]
                    placed[tile, pl.ds(row * BLOCK + half, packs, stride=2), :] = block * mask
        for tile in range(2):
            pd[:, tile * wide : (tile + 1) * wide] = placed[tile].astype(jnp.bfloat16)

    place(panels[0])
    own_t[...] = pd[...].astype(jnp.float32).T.astype(jnp.bfloat16)

    def one_step(step, carry):
        index = offset_of(step) + window // 2
        slab_copy(step).wait()

        def one_row(g, inner):
            first = pl.multiple_of(g * BLOCK, BLOCK)
            totals = [None] * columns
            for k in range(pairs):
                tile = a_slabs[step, pl.ds(first, BLOCK), k * wide : (k + 1) * wide].astype(jnp.float32)
                for side, values in enumerate((tile, pltpu.roll(tile, BLOCK, 1))):
                    code = codes[index, g, 2 * k + side]
                    grouped = values.reshape(BLOCK // 8, 8, wide)
                    for m in range(columns):
                        weight = jnp.where(code == upper + 2.0 * m, 1.0, 0.0)
                        term = grouped * weight[None]
                        totals[m] = term if totals[m] is None else totals[m] + term
            for m in range(columns):
                spread[pl.ds(first, BLOCK), m * wide : (m + 1) * wide] = (
                    totals[m].reshape(BLOCK, wide).astype(jnp.bfloat16)
                )
            return inner

        lax.fori_loop(0, rows, one_row, 0)

        @pl.when(step > 0)
        def _():
            panel_copy(step).wait_recv()
            place(panels[step])

        product = jnp.dot(spread[...], pd[...], preferred_element_type=jnp.float32)
        top = product.astype(jnp.bfloat16)
        rest = (product - top.astype(jnp.float32)).astype(jnp.bfloat16)
        coarse = jnp.dot(own_t[...], top, preferred_element_type=jnp.float32)
        coarse = coarse + jnp.dot(own_t[...], rest, preferred_element_type=jnp.float32)
        for q in range(n_partner):
            part = jnp.concatenate(
                [coarse[i * BLOCK + q * height : i * BLOCK + (q + 1) * height] for i in range(AGG)], axis=0
            )
            parts[step, q] = part
            sent[step, q] = part.astype(jnp.bfloat16)
        for d in range(1, n_partner):
            part_copy(step, d).start()
        return carry

    lax.fori_loop(0, window, one_step, 0)

    def finish(step, carry):
        index = offset_of(step) + window // 2
        total = parts[step, mine]
        for d in range(1, n_partner):
            part_copy(step, d).wait_recv()
            total = total + got[step, d - 1].astype(jnp.float32)
        start = pl.multiple_of(index * WIDE, WIDE)
        for i in range(AGG):
            out_ref[i, :, pl.ds(start, WIDE)] = total[i * height : (i + 1) * height]
        return carry

    lax.fori_loop(0, window, finish, 0)
    for step in range(1, window):
        panel_copy(step).wait_send()
    for step in range(window):
        for d in range(1, n_partner):
            part_copy(step, d).wait_send()


def on_device(n_blk, n_partner, a_blocks, p_blocks, agg_ids, cols, counts):
    rows = p_blocks.shape[0]
    window = counts.shape[1]
    kper = cols.shape[1] // window
    height = BLOCK // n_partner
    vmem = pl.BlockSpec(memory_space=pltpu.VMEM)
    size = rows * BLOCK
    others = max(n_partner - 1, 1)
    panel_rows = rows * BLOCK // 2 + 2 * rows
    return pl.pallas_call(
        functools.partial(kernel, n_blk, n_partner, rows, window, kper),
        out_shape=jax.ShapeDtypeStruct((AGG, height, window * WIDE), jnp.float32),
        in_specs=[pl.BlockSpec(memory_space=pltpu.HBM), vmem, pl.BlockSpec(memory_space=pltpu.SMEM), vmem, vmem],
        out_specs=vmem,
        scratch_shapes=[
            pltpu.VMEM((window, size, kper * BLOCK), jnp.bfloat16),
            pltpu.VMEM((window, panel_rows, 2 * BLOCK), jnp.bfloat16),
            pltpu.VMEM((window, rows, kper, 8, 2 * BLOCK), jnp.float32),
            pltpu.VMEM((rows, BLOCK // 2, 2 * BLOCK), jnp.float32),
            pltpu.VMEM((WIDE, size), jnp.bfloat16),
            pltpu.VMEM((size, size), jnp.bfloat16),
            pltpu.VMEM((2, size, 2 * BLOCK), jnp.float32),
            pltpu.VMEM((size, WIDE), jnp.bfloat16),
            pltpu.VMEM((window, n_partner, AGG * height, WIDE), jnp.float32),
            pltpu.VMEM((window, n_partner, AGG * height, WIDE), jnp.bfloat16),
            pltpu.VMEM((window, others, AGG * height, WIDE), jnp.bfloat16),
            pltpu.SemaphoreType.DMA((window,)),
            pltpu.SemaphoreType.DMA((window,)),
            pltpu.SemaphoreType.DMA((window,)),
            pltpu.SemaphoreType.DMA((window, others)),
            pltpu.SemaphoreType.DMA((window, others)),
        ],
        compiler_params=pltpu.CompilerParams(
            collective_id=0, has_side_effects=True, vmem_limit_bytes=60 * 1024 * 1024
        ),
        cost_estimate=pl.CostEstimate(flops=3 * 10**9, bytes_accessed=5 * 10**6, transcendentals=0),
    )(a_blocks, p_blocks, agg_ids, cols, counts)


def solution(mesh):
    placed = (
        P(("blk", "partner"), None),
        P(("blk", "partner"), None),
        P(("blk", "partner")),
        P(("blk", "partner"), None),
        P(("blk", "partner"), None),
    )
    return jax.shard_map(
        functools.partial(on_device, mesh.shape["blk"], mesh.shape["partner"]),
        mesh=mesh, in_specs=placed, out_specs=P("blk", "partner", None), check_vma=False,
    )
```

time: 33.2 us -> 29.8 us (0.90)
  local copies, waits for them, and re-layouts: 7.08 us -> 2.3 us
  Pallas kernels: 24.9 us -> 27.3 us
  other arithmetic: 0.87 us -> 0 us
    reshape x6 -> x0, local copies, waits for them, and re-layouts: 3.46 us -> none  [the longest x1 1.34 us: on_device(): code = jnp.repeat(code, BLOCK, axis=2)]
    pallas_call x1, Pallas kernels: 24.9 us -> 27.3 us  [on_device(): pl.pallas_call(functools.partial(kernel, n_blk, n_partner, rows, window,...]
    broadcast_in_dim x1 -> x0, local copies, waits for them, and re-layouts: 1.4 us -> none  [on_device(): code = jnp.repeat(code, BLOCK, axis=2)]
    unnamed x4 -> x1, local copies, waits for them, and re-layouts: 1.15 us -> 2.3 us
    eq x2 -> x0, local copies, waits for them, and re-layouts: 0.89 us -> none  [on_device(): agg_ids[None, :, None] == lane.reshape(2, 1, 2 * BLOCK)]
    transpose x1 -> x0, other arithmetic: 0.76 us -> none  [on_device(): code = code.transpose(1, 0, 2).reshape(window * rows, pairs, 2)]
where the time goes in v1:
time: 29.8 us; the launch traced here: 29.6 us
  Pallas kernels  27.3 us (92%)
  local copies, waits for them, and re-layouts  2.3 us (8%)
    pallas_call x1, Pallas kernels, on_device(): pl.pallas_call(functools.partial(kernel, n_blk, n_partner, rows, window,...  27.3 us
    unnamed x1, local copies, waits for them, and re-layouts  2.3 us

profile of v1, /device:TPU:0, one launch (start us, length us, event | category | flops | bytes accessed | tf_op | source)
XLA Modules:
  0.0 29.6 jit_solution(2149078056382430753)
XLA Ops:
  0.0 27.3 %shard_map.55 = f32[4,32,2048]{2,1,0:T(8,128)} custom-call(bf16[512,3072]{1,0:T(8,128)(2,1)} %a_ref.1, bf16[8,4096]{1,0:T(8,128)(2,1)} %p_ref.1, s32[8]{0:T(128)} %agg_ref.1, s32[8,48]{1,0:T(8,128)} %cols_ref.1, s32[8,8]{1,0:T(8,128)} %counts_ref.1), custom_call_target="tpu_custom_call" | custom-call | flops 3000000000 | bytes 5000000 | tf_op jit(solution)/shard_map/pallas_call | solution.py:195
  27.3 2.3 %copy.7 = f32[4,32,2048]{2,1,0:T(8,128)} copy(f32[4,32,2048]{2,1,0:T(8,128)} %shard_map.55) | data formatting | bytes 2097152

commit v2 on v1

--- a/solution.py
+++ b/solution.py
@@ -140,10 +140,9 @@
                 )
             return inner
 
-        lax.fori_loop(0, rows, one_row, 0)
-
-        @pl.when(step > 0)
-        def _():
+        lax.fori_loop(0, rows, one_row, 0, unroll=4)
+
+        if type(step) is not int:
             panel_copy(step).wait_recv()
             place(panels[step])
 
@@ -162,7 +161,8 @@
             part_copy(step, d).start()
         return carry
 
-    lax.fori_loop(0, window, one_step, 0)
+    one_step(0, 0)
+    lax.fori_loop(1, window, one_step, 0)
 
     def finish(step, carry):
         index = offset_of(step) + window // 2

time: 29.8 us -> 27.5 us (0.923)
  Pallas kernels: 27.3 us -> 25 us
    pallas_call x1, Pallas kernels: 27.3 us -> 25 us  [on_device(): pl.pallas_call(functools.partial(kernel, n_blk, n_partner, rows, window,...]
where the time goes in v2:
time: 27.5 us; the launch traced here: 27.3 us
  Pallas kernels  25 us (91%)
  local copies, waits for them, and re-layouts  2.3 us (8%)
    pallas_call x1, Pallas kernels, on_device(): pl.pallas_call(functools.partial(kernel, n_blk, n_partner, rows, window,...  25 us
    unnamed x1, local copies, waits for them, and re-layouts  2.3 us

profile of v2, /device:TPU:0, one launch (start us, length us, event | category | flops | bytes accessed | tf_op | source)
XLA Modules:
  0.0 27.3 jit_solution(13737114210988335617)
XLA Ops:
  0.0 25.0 %shard_map.55 = f32[4,32,2048]{2,1,0:T(8,128)} custom-call(bf16[512,3072]{1,0:T(8,128)(2,1)} %a_ref.1, bf16[8,4096]{1,0:T(8,128)(2,1)} %p_ref.1, s32[8]{0:T(128)} %agg_ref.1, s32[8,48]{1,0:T(8,128)} %cols_ref.1, s32[8,8]{1,0:T(8,128)} %counts_ref.1), custom_call_target="tpu_custom_call" | custom-call | flops 3000000000 | bytes 5000000 | tf_op jit(solution)/shard_map/pallas_call | solution.py:195
  25.0 2.3 %copy.7 = f32[4,32,2048]{2,1,0:T(8,128)} copy(f32[4,32,2048]{2,1,0:T(8,128)} %shard_map.55) | data formatting | bytes 2097152

commit v3 on v2

--- a/solution.py
+++ b/solution.py
@@ -149,8 +149,8 @@
         product = jnp.dot(spread[...], pd[...], preferred_element_type=jnp.float32)
         top = product.astype(jnp.bfloat16)
         rest = (product - top.astype(jnp.float32)).astype(jnp.bfloat16)
-        coarse = jnp.dot(own_t[...], top, preferred_element_type=jnp.float32)
-        coarse = coarse + jnp.dot(own_t[...], rest, preferred_element_type=jnp.float32)
+        both = jnp.dot(own_t[...], jnp.concatenate([top, rest], axis=1), preferred_element_type=jnp.float32)
+        coarse = both[:, :WIDE] + both[:, WIDE:]
         for q in range(n_partner):
             part = jnp.concatenate(
                 [coarse[i * BLOCK + q * height : i * BLOCK + (q + 1) * height] for i in range(AGG)], axis=0

time: 27.5 us -> 27.5 us (level)
  no operation moved by 1% of the time
where the time goes in v3:
time: 27.5 us; the launch traced here: 27.3 us
  Pallas kernels  25 us (91%)
  local copies, waits for them, and re-layouts  2.3 us (8%)
    pallas_call x1, Pallas kernels, on_device(): pl.pallas_call(functools.partial(kernel, n_blk, n_partner, rows, window,...  25 us
    unnamed x1, local copies, waits for them, and re-layouts  2.3 us

profile of v3, /device:TPU:0, one launch (start us, length us, event | category | flops | bytes accessed | tf_op | source)
XLA Modules:
  0.0 27.3 jit_solution(13413817151821936119)
XLA Ops:
  0.0 25.0 %shard_map.55 = f32[4,32,2048]{2,1,0:T(8,128)} custom-call(bf16[512,3072]{1,0:T(8,128)(2,1)} %a_ref.1, bf16[8,4096]{1,0:T(8,128)(2,1)} %p_ref.1, s32[8]{0:T(128)} %agg_ref.1, s32[8,48]{1,0:T(8,128)} %cols_ref.1, s32[8,8]{1,0:T(8,128)} %counts_ref.1), custom_call_target="tpu_custom_call" | custom-call | flops 3000000000 | bytes 5000000 | tf_op jit(solution)/shard_map/pallas_call | solution.py:195
  25.0 2.3 %copy.7 = f32[4,32,2048]{2,1,0:T(8,128)} copy(f32[4,32,2048]{2,1,0:T(8,128)} %shard_map.55) | data formatting | bytes 2097152

commit v4 on v2

--- a/solution.py
+++ b/solution.py
@@ -162,7 +162,7 @@
         return carry
 
     one_step(0, 0)
-    lax.fori_loop(1, window, one_step, 0)
+    lax.fori_loop(1, window, one_step, 0, unroll=True)
 
     def finish(step, carry):
         index = offset_of(step) + window // 2

time: 27.5 us -> 27.4 us (level)
  no operation moved by 1% of the time
where the time goes in v4:
time: 27.4 us; the launch traced here: 27.3 us
  Pallas kernels  24.9 us (91%)
  local copies, waits for them, and re-layouts  2.3 us (8%)
    pallas_call x1, Pallas kernels, on_device(): pl.pallas_call(functools.partial(kernel, n_blk, n_partner, rows, window,...  24.9 us
    unnamed x1, local copies, waits for them, and re-layouts  2.3 us

profile of v4, /device:TPU:0, one launch (start us, length us, event | category | flops | bytes accessed | tf_op | source)
XLA Modules:
  0.0 27.3 jit_solution(6994463843071351637)
XLA Ops:
  0.0 24.9 %shard_map.55 = f32[4,32,2048]{2,1,0:T(8,128)} custom-call(bf16[512,3072]{1,0:T(8,128)(2,1)} %a_ref.1, bf16[8,4096]{1,0:T(8,128)(2,1)} %p_ref.1, s32[8]{0:T(128)} %agg_ref.1, s32[8,48]{1,0:T(8,128)} %cols_ref.1, s32[8,8]{1,0:T(8,128)} %counts_ref.1), custom_call_target="tpu_custom_call" | custom-call | flops 3000000000 | bytes 5000000 | tf_op jit(solution)/shard_map/pallas_call | solution.py:195
  25.0 2.3 %copy.7 = f32[4,32,2048]{2,1,0:T(8,128)} copy(f32[4,32,2048]{2,1,0:T(8,128)} %shard_map.55) | data formatting | bytes 2097152
